TPU v7x, 32 devices: a whole 2x2x4 slice. The times are simulated.
32 devices in a mesh: parts: 2 (over x), date: 16 (over z, y, core).
Axes of the slice: x: 2, y: 2, z: 4, core: 2. Of those that a mesh axis runs over, the one named last changes fastest.
Arguments:
- slave_acquisitions: bfloat16 [32, 2, 192, 2112], P(('parts', 'date')), parts along dimension 0, may hold values from -6 to 6
- master_subswath_crop: bfloat16 [2, 256, 2048], P(None, 'parts', 'date'), parts along dimension 1, may hold values from -6 to 6
- deskew_angular_slope: float32 [2048], P('date'), may hold values from 4 to 40
- deskew_central_epoch: float32 [2048], P('date'), may hold values from 0.2 to 0.8
- along_track_whole_row: int32 [32, 128], P(('parts', 'date')), parts along dimension 0, may hold values from 3 to 134, as said below
- along_track_subpixel: float32 [32, 128], P(('parts', 'date')), parts along dimension 0, may hold values from 0 to 1
- along_track_strip_opening: int32 [32, 1], P(('parts', 'date')), parts along dimension 0, may hold values from 0 to 0
- slant_whole_column: int32 [32, 2048], P(('parts', 'date')), parts along dimension 0, may hold values from 3 to 2054, as said below
- slant_subpixel: float32 [32, 2048], P(('parts', 'date')), parts along dimension 0, may hold values from 0 to 1
- slant_strip_opening: int32 [32, 16], P(('parts', 'date')), parts along dimension 0, may hold values from 0 to 1920
Outputs:
- interferogram: float32 [32, 2, 32, 128], P(('parts', 'date')), parts along dimension 0
- stack_power: float32 [64, 128], P('parts'), parts along dimension 0
There are 2 independent parts, one for each index of `parts`. A program takes and returns all parts, laid end to end along the dimension named above; an argument that names none is the same for every part. Nothing has to cross between parts.
Inputs may be any that keep to these rules, and one draw needn't show every extreme that they name: For every date and every output line i of block b = i // 128, the lines along_track_whole_row - 3 to along_track_whole_row + 4 lie within along_track_strip_opening[b] to along_track_strip_opening[b] + 191. For every date and every output sample c of block b = c // 128, the samples slant_whole_column - 3 to slant_whole_column + 4 lie within slant_strip_opening[b] to slant_strip_opening[b] + 191.
All inputs are finite; a program needn't handle non-finite values.
Results may differ from a plain program's by a relative error of at most 0.0051.
Values may be sent and summed in bfloat16 or wider, within the bound.
A program may use at most 128 MiB of HBM per device.

v0:
```python
import math

import jax
import jax.numpy as jnp
from jax import lax
from jax.sharding import PartitionSpec as P

TAPS = 8
BLK = 128
WIN = 192
LOOK_AZ = 4
LOOK_RG = 16


epsilon = 1e-06


def kernel_weights(fraction):
    tap_offsets = jnp.arange(TAPS, dtype=jnp.float32) - (TAPS // 2 - 1)
    spacing = tap_offsets[None, :] - fraction[:, None]
    return jnp.sinc(spacing) * (0.5 + 0.5 * jnp.cos(jnp.pi * spacing / (TAPS // 2)))


def tap_block(positions, weights, first_cell):
    tap_steps = jnp.arange(TAPS, dtype=jnp.int32) - (TAPS // 2 - 1)
    target = positions[:, None] + tap_steps[None, :] - first_cell
    window_cells = jnp.arange(WIN, dtype=jnp.int32)
    matches = (target[:, :, None] == window_cells[None, None, :]).astype(jnp.float32)
    return jnp.sum(weights[:, :, None] * matches, axis=1).astype(jnp.bfloat16)


def look_sums(values):
    leading = values.shape[:-2]
    shaped = values.reshape(
        leading + (values.shape[-2] // LOOK_AZ, LOOK_AZ, values.shape[-1] // LOOK_RG, LOOK_RG)
    )
    return shaped.sum(axis=(-3, -1))


def range_section(second_date, col_pos, col_frac, col_band, rate_all, center_all):
    lines_in = second_date.shape[1]
    samples = rate_all.shape[0]
    blocks_all = samples // BLK
    group_size = math.gcd(blocks_all, 8)
    line_time = jnp.arange(lines_in, dtype=jnp.float32) / lines_in
    range_weights = kernel_weights(col_frac)
    output = jnp.zeros((2, lines_in, samples), jnp.bfloat16)

    def range_turn(turn_index, output):
        first_block = turn_index * group_size
        first_column = first_block * BLK
        starts = lax.dynamic_slice_in_dim(col_band, first_block, group_size)
        windows = jax.vmap(lambda offset: lax.dynamic_slice_in_dim(second_date, offset, WIN, 2))(
            starts
        )
        columns = lax.dynamic_slice_in_dim(col_pos, first_column, group_size * BLK).reshape(
            group_size, BLK
        )
        weights = lax.dynamic_slice_in_dim(
            range_weights, first_column, group_size * BLK, 0
        ).reshape(group_size, BLK, TAPS)
        tap_matrix = jax.vmap(tap_block)(columns, weights, starts)
        ranged = jnp.einsum(
            "gpjw,gcw->gpjc", windows, tap_matrix, preferred_element_type=jnp.float32
        )
        rate_block = lax.dynamic_slice_in_dim(rate_all, first_column, group_size * BLK).reshape(
            group_size, 1, BLK
        )
        center_block = lax.dynamic_slice_in_dim(center_all, first_column, group_size * BLK).reshape(
            group_size, 1, BLK
        )
        offsets = line_time[None, :, None] - center_block
        phases = rate_block * offsets * offsets
        cosine = jnp.cos(phases)
        sine_part = jnp.sin(phases)
        real_part = ranged[:, 0] * cosine + ranged[:, 1] * sine_part
        imag_part = ranged[:, 1] * cosine - ranged[:, 0] * sine_part
        new_block = jnp.stack([real_part, imag_part], axis=0).astype(jnp.bfloat16)
        new_block = jnp.transpose(new_block, (0, 2, 1, 3)).reshape(2, lines_in, group_size * BLK)
        return lax.dynamic_update_slice_in_dim(output, new_block, first_column, 2)

    return lax.fori_loop(0, blocks_all // group_size, range_turn, output)


def azimuth_section(deramped, row_pos, row_frac, row_band, rate_all, center_all):
    lines_in = deramped.shape[1]
    samples = deramped.shape[2]
    lines_out = row_pos.shape[0]
    azimuth_weights = kernel_weights(row_frac)
    position = row_pos.astype(jnp.float32) + row_frac
    output = jnp.zeros((2, lines_out, samples), jnp.bfloat16)

    def azimuth_turn(block_index, output):
        first_cell = row_band[block_index]
        weights = lax.dynamic_slice_in_dim(azimuth_weights, block_index * BLK, BLK, 0)
        tap_matrix = tap_block(row_pos, weights, first_cell)
        moved = jnp.einsum("iw,pwc->pic", tap_matrix, deramped, preferred_element_type=jnp.float32)
        place_time = position / lines_in
        offsets = place_time[:, None] - center_all[None, :]
        phases = rate_all[None, :] * offsets * offsets
        cosine = jnp.cos(phases)
        sine_part = jnp.sin(phases)
        real_part = moved[0] * cosine - moved[1] * sine_part
        imag_part = moved[0] * sine_part + moved[1] * cosine
        new_block = jnp.stack([real_part, imag_part]).astype(jnp.bfloat16)
        return lax.dynamic_update_slice_in_dim(output, new_block, block_index * BLK, 1)

    return lax.fori_loop(0, lines_out // BLK, azimuth_turn, output)


def per_device(
    slave_acquisitions,
    master_subswath_crop,
    deskew_angular_slope,
    deskew_central_epoch,
    along_track_whole_row,
    along_track_subpixel,
    along_track_strip_opening,
    slant_whole_column,
    slant_subpixel,
    slant_strip_opening,
):
    rate_all, center_all = (
        lax.all_gather(deskew_angular_slope, "date", axis=0, tiled=True),
        lax.all_gather(deskew_central_epoch, "date", axis=0, tiled=True),
    )
    deramped = range_section(
        slave_acquisitions[0],
        slant_whole_column[0],
        slant_subpixel[0],
        slant_strip_opening[0],
        rate_all,
        center_all,
    )
    resampled = azimuth_section(
        deramped,
        along_track_whole_row[0],
        along_track_subpixel[0],
        along_track_strip_opening[0],
        rate_all,
        center_all,
    )
    look_count = LOOK_AZ * LOOK_RG
    master_tile = lax.all_gather(master_subswath_crop, "date", axis=2, tiled=True)
    span_width = master_tile.shape[2]
    local_part = resampled.astype(jnp.float32)
    master_pixel_values = master_tile.astype(jnp.float32)
    real_part = master_pixel_values[0] * local_part[0] + master_pixel_values[1] * local_part[1]
    imag_part = master_pixel_values[1] * local_part[0] - master_pixel_values[0] * local_part[1]
    ref_energy = (
        master_pixel_values[0] * master_pixel_values[0]
        + master_pixel_values[1] * master_pixel_values[1]
    )
    term_stack = jnp.stack([real_part, imag_part, ref_energy])
    looked = term_stack.reshape(3, term_stack.shape[1] // LOOK_AZ, LOOK_AZ, span_width).sum(axis=2)
    looked = (
        looked.reshape(3, looked.shape[1], looked.shape[2] // LOOK_RG, LOOK_RG).sum(axis=3)
        / look_count
    )
    real_sec = resampled[0].astype(jnp.float32)
    imag_sec = resampled[1].astype(jnp.float32)
    sec_power = look_sums(real_sec * real_sec + imag_sec * imag_sec) / look_count
    normalizer = 1.0 / jnp.sqrt(looked[2] * sec_power + epsilon)
    interferogram = jnp.stack([looked[0] * normalizer, looked[1] * normalizer])[None]
    stack_power = lax.psum(sec_power, "date") / lax.axis_size("date")
    return (interferogram, stack_power)


def solution(mesh):
    placed = (
        P(("parts", "date"), None, None, None),
        P(None, "parts", "date"),
        P("date"),
        P("date"),
        P(("parts", "date"), None),
        P(("parts", "date"), None),
        P(("parts", "date"), None),
        P(("parts", "date"), None),
        P(("parts", "date"), None),
        P(("parts", "date"), None),
    )
    return jax.shard_map(
        per_device,
        mesh=mesh,
        in_specs=placed,
        out_specs=(P(("parts", "date"), None, None, None), P("parts", None)),
        check_vma=False,
    )
```

profile of v0, /device:TPU:0, one launch (start us, length us, event | category | flops | bytes accessed | tf_op | source)
XLA Modules:
  0.0 181.5 jit_solution(5359628935122754498)
XLA Ops:
  7.2 0.7 all-gather.4.cloned.1.call-update
  9.1 23.2 %all-gather = f32[16,1,128]{2,1,0:T(1,128)S(1)} all-gather(f32[1,1,128]{2,1,0:T(1,128)} %bitcast.86), channel_id=1, replica_groups=mesh['parts'=2,'date'=16] {'date'}, dimensions={0}, use_global_device_ids=true | all-gather | bytes 8704 | tf_op jit(solution)/shard_map/all_gather | solution.py:124
  32.3 17.5 %all-gather.1 = f32[16,1,128]{2,1,0:T(1,128)S(1)} all-gather(f32[1,1,128]{2,1,0:T(1,128)} %bitcast.87), channel_id=1, replica_groups=mesh['parts'=2,'date'=16] {'date'}, dimensions={0}, use_global_device_ids=true | all-gather | bytes 8704 | tf_op jit(solution)/shard_map/all_gather | solution.py:125
  49.7 1.4 fusion.48
  51.1 1.1 fusion.17
  52.2 6.6 %copy.41 = bf16[1,2,192,2112]{2,1,3,0:T(2,128)(2,1)} copy(bf16[1,2,192,2112]{3,2,1,0:T(8,128)(2,1)} %param.12) | data formatting | bytes 3244032 | tf_op args[0]
  58.9 23.4 %while.21 = (s32[]{:T(128)}, bf16[2,192,2048]{2,1,0:T(8,128)(2,1)S(1)}, s32[16]{0:T(128)S(1)}, bf16[2,192,2112]{1,0,2:T(2,128)(2,1)}, s32[2048]{0:T(1024)}, /*in...) while((s32[]{:T(128)}, ...), condition=%wide.region_2.3_spmd.clone, body=%wide.region_0.2_spmd.clone.sunk | while | flops 158089472 | bytes 10689001 | solution.py:82
  59.1 0.7 dynamic-slice_bitcast_fusion.8
  59.9 1.1 select_reduce_fusion.3
  60.9 5.3 %gather_fusion = bf16[8,2,192,192]{2,1,3,0:T(2,128)(2,1)S(1)} fusion(bf16[2,192,2112]{1,0,2:T(2,128)(2,1)} %get-tuple-element.403, s32[8]{0:T(128)S(1)} %get-tuple-element.365), kind=kCustom, calls=%fused_computation.clone.clone.1 | custom fusion | bytes 2359392 | tf_op jit(solution)/shard_map/while/body/eval_jaxpr/vmap()/gather | solution.py:53
  66.3 0.7 fusion.78
  67.0 3.4 %add_convert_fusion.4 = (bf16[1,8,192,128]{3,2,1,0:T(8,128)(2,1)S(1)}, bf16[1,8,192,128]{3,2,1,0:T(8,128)(2,1)S(1)}) fusion(f32[8,2,192,128]{3,2,1,0:T(8,128)S(1)} %fusion.78, f32[8,128]{1,0:T(8,128)S(1)} %get-tuple-element.368, f32[192]{0:T(256)S(1)} %iota_multiply_fusion.2, f32[8,128]{1,0:T(8,128)S(1)} %get-tuple-element.369), kind=kLoop, calls=%fused_computation.12.clone.1 | loop fusion | flops 2162688 | bytes 2368256 | tf_op jit(solution)/shard_map/convert
  70.8 0.7 dynamic-slice_bitcast_fusion.8
  71.6 1.1 select_reduce_fusion.3
  72.7 5.3 %gather_fusion = bf16[8,2,192,192]{2,1,3,0:T(2,128)(2,1)S(1)} fusion(bf16[2,192,2112]{1,0,2:T(2,128)(2,1)} %get-tuple-element.403, s32[8]{0:T(128)S(1)} %get-tuple-element.365), kind=kCustom, calls=%fused_computation.clone.clone.1 | custom fusion | bytes 2359392 | tf_op jit(solution)/shard_map/while/body/eval_jaxpr/vmap()/gather | solution.py:53
  78.0 0.7 fusion.78
  78.7 3.4 %add_convert_fusion.4 = (bf16[1,8,192,128]{3,2,1,0:T(8,128)(2,1)S(1)}, bf16[1,8,192,128]{3,2,1,0:T(8,128)(2,1)S(1)}) fusion(f32[8,2,192,128]{3,2,1,0:T(8,128)S(1)} %fusion.78, f32[8,128]{1,0:T(8,128)S(1)} %get-tuple-element.368, f32[192]{0:T(256)S(1)} %iota_multiply_fusion.2, f32[8,128]{1,0:T(8,128)S(1)} %get-tuple-element.369), kind=kLoop, calls=%fused_computation.12.clone.1 | loop fusion | flops 2162688 | bytes 2368256 | tf_op jit(solution)/shard_map/convert
  82.3 0.7 add_subtract_fusion.1
  83.1 0.8 select_reduce_fusion.1
  85.0 5.1 %multiply_add_fusion = (f32[1,128,2048]{2,1,0:T(8,128)S(1)}, bf16[1,128,2048]{2,1,0:T(8,128)(2,1)}, bf16[1,128,2048]{2,1,0:T(8,128)(2,1)}) fusion(f32[2,128,2048]{2,1,0:T(8,128)S(1)} %convolution_bitcast_fusion, f32[2048]{0:T(1024)S(1)} %get-tuple-element.427, f32[128]{0:T(128)S(1)} %add_multiply_fusion, f32[2048]{0:T(1024)S(1)} %get-tuple-element.426), kind=kLoop, calls=%fused_computation.32 | loop fusion | flops 4194304 | bytes 4211200 | tf_op jit(solution)/shard_map/add | solution.py:162
  90.1 4.8 %add.393 = f32[32,4,128,16]{3,2,1,0:T(8,128)} reshape(f32[1,128,2048]{2,1,0:T(8,128)S(1)} %get-tuple-element.296) | data formatting | bytes 2097152 | tf_op jit(solution)/shard_map/add | solution.py:162
  95.0 4.1 %reduce_sum.56 = f32[32,128]{1,0:T(8,128)S(1)} reduce(f32[32,4,128,16]{3,2,1,0:T(8,128)} %add.393, f32[]{:T(128)} %constant.194.clone.1), dimensions={1,3}, to_apply=%region_6.7 | reduce | flops 258048 | bytes 1064964 | tf_op jit(solution)/shard_map/reduce_sum | solution.py:37
  99.2 59.2 %psum.7 = f32[32,128]{0,1:T(8,128)S(1)} all-reduce(f32[32,128]{0,1:T(8,128)S(1)} %broadcast_multiply_fusion.2), channel_id=1, replica_groups=mesh['parts'=2,'date'=16] {'date'}, use_global_device_ids=true, to_apply=%region_7.8 | all-reduce | flops 4096 | bytes 32768 | tf_op jit(solution)/shard_map/psum | solution.py:165
  158.4 0.7 copy.46
  159.2 1.5 convert_element_type.70
  160.7 1.8 %multiply_add_fusion.2 = (f32[1,128,2048]{2,1,0:T(8,128)}, f32[1,128,2048]{2,1,0:T(8,128)}, f32[1,128,2048]{2,1,0:T(8,128)S(1)}) fusion(f32[2,128,2048]{2,1,0:T(8,128)S(1)} %maximum_convert_fusion, f32[2,128,2048]{2,1,0:T(8,128)S(1)} %convert_element_type.70), kind=kLoop, calls=%fused_computation.35 | loop fusion | flops 2359296 | bytes 7340032 | tf_op jit(solution)/shard_map/add | solution.py:148
  162.5 1.6 stack.44
  164.1 1.3 stack.45
  165.4 1.3 stack.46
  166.7 4.4 %maximum_reduce_fusion = f32[3,32,2048]{2,1,0:T(8,128)} fusion(f32[1,32,4,2048]{3,2,1,0:T(4,128)} %stack.46, f32[1,32,4,2048]{3,2,1,0:T(4,128)S(1)} %copy-done.1, f32[1,32,4,2048]{3,2,1,0:T(4,128)S(1)} %stack.44), kind=kLoop, calls=%fused_computation.27 | loop fusion | flops 2162688 | bytes 3932160 | tf_op jit(solution)/shard_map/reduce_sum | solution.py:155
  171.1 2.0 %copy.42 = f32[3,32,2048]{1,2,0:T(8,128)S(1)} copy(f32[3,32,2048]{2,1,0:T(8,128)} %maximum_reduce_fusion) | data formatting | bytes 1572864 | tf_op jit(solution)/shard_map/reduce_sum | solution.py:155
  173.1 0.7 bitcast_reduce_fusion
  (66 shorter events, 3.8 us)
Async XLA Ops:
  7.2 152.0 %all-gather.4.cloned.1.call-start = ((), (), s32[]{:S(2)}) async-start(), calls=%async_computation | async-start | bytes 1114112 | tf_op jit(solution)/shard_map/all_gather | solution.py:144
  52.2 6.8 %copy-start.10 = (s32[1,16]{1,0:T(1,128)S(1)}, s32[1,16]{1,0:T(1,128)}, u32[]{:S(2)}) copy-start(s32[1,16]{1,0:T(1,128)} %param.21) | copy-start | bytes 196
  58.9 0.9 copy-start.4
  58.9 0.9 copy-start.6
  58.9 0.9 copy-start.8
  67.0 3.6 %copy-start.5 = (f32[2048,8]{0,1:T(8,128)S(1)}, f32[2048,8]{0,1:T(8,128)}, u32[]{:S(2)}) copy-start(f32[2048,8]{0,1:T(8,128)} %copy-done.4) | copy-start | bytes 196612 | tf_op jit(solution)/shard_map/while
  67.0 3.6 %copy-start.7 = (f32[2048]{0:T(1024)S(1)}, f32[2048]{0:T(1024)}, u32[]{:S(2)}) copy-start(f32[2048]{0:T(1024)} %copy-done.6) | copy-start | bytes 24580 | tf_op jit(solution)/shard_map/while
  67.0 3.6 %copy-start.9 = (f32[2048]{0:T(1024)S(1)}, f32[2048]{0:T(1024)}, u32[]{:S(2)}) copy-start(f32[2048]{0:T(1024)} %copy-done.8) | copy-start | bytes 24580 | tf_op jit(solution)/shard_map/while
  67.0 3.6 %copy-start.11 = (s32[1,16]{1,0:T(1,128)S(1)}, s32[1,16]{1,0:T(1,128)}, u32[]{:S(2)}) copy-start(s32[1,16]{1,0:T(1,128)} %get-tuple-element.434) | copy-start | bytes 196 | tf_op jit(solution)/shard_map/while
  70.6 0.9 copy-start.4
  70.6 0.9 copy-start.6
  70.7 0.9 copy-start.8
  78.7 3.6 %copy-start.5 = (f32[2048,8]{0,1:T(8,128)S(1)}, f32[2048,8]{0,1:T(8,128)}, u32[]{:S(2)}) copy-start(f32[2048,8]{0,1:T(8,128)} %copy-done.4) | copy-start | bytes 196612 | tf_op jit(solution)/shard_map/while
  78.7 3.6 %copy-start.7 = (f32[2048]{0:T(1024)S(1)}, f32[2048]{0:T(1024)}, u32[]{:S(2)}) copy-start(f32[2048]{0:T(1024)} %copy-done.6) | copy-start | bytes 24580 | tf_op jit(solution)/shard_map/while
  78.7 3.6 %copy-start.9 = (f32[2048]{0:T(1024)S(1)}, f32[2048]{0:T(1024)}, u32[]{:S(2)}) copy-start(f32[2048]{0:T(1024)} %copy-done.8) | copy-start | bytes 24580 | tf_op jit(solution)/shard_map/while
  78.7 3.6 %copy-start.11 = (s32[1,16]{1,0:T(1,128)S(1)}, s32[1,16]{1,0:T(1,128)}, u32[]{:S(2)}) copy-start(s32[1,16]{1,0:T(1,128)} %get-tuple-element.434) | copy-start | bytes 196 | tf_op jit(solution)/shard_map/while
  95.0 64.1 %copy-start.2 = (bf16[1,128,2048]{2,1,0:T(8,128)(2,1)S(1)}, bf16[1,128,2048]{2,1,0:T(8,128)(2,1)}, u32[]{:S(2)}) copy-start(bf16[1,128,2048]{2,1,0:T(8,128)(2,1)} %get-tuple-element.297) | copy-start | bytes 1572868
  95.0 64.1 %copy-start.3 = (bf16[1,128,2048]{2,1,0:T(8,128)(2,1)S(1)}, bf16[1,128,2048]{2,1,0:T(8,128)(2,1)}, u32[]{:S(2)}) copy-start(bf16[1,128,2048]{2,1,0:T(8,128)(2,1)} %get-tuple-element.298) | copy-start | bytes 1572868
  162.5 1.6 copy-start
  165.4 1.3 copy-start.1
Sparse Core Ops, SparseCore 0:
  10.2 39.5 all-gather.3
where the time goes:
time: 182 us; the launch traced here: 181 us
  blocking collectives  99.8 us (55%)
  other arithmetic  33.2 us (18%)
  local copies, waits for them, and re-layouts  30.8 us (17%)
  between operations  14.8 us (8%)
  matrix products  1.87 us (1%)
    psum x1, blocking collectives, per_device(): stack_power = lax.psum(sec_power, 'date') / lax.axis_size('date')  59.2 us
    all_gather x1, blocking collectives, per_device(): lax.all_gather(deskew_angular_slope, 'date', axis=0, tiled=True)  23.2 us
    all_gather x1, blocking collectives, per_device(): lax.all_gather(deskew_central_epoch, 'date', axis=0, tiled=True)  17.5 us
    gather x2, local copies, waits for them, and re-layouts, range_turn(): lax.dynamic_slice_in_dim(second_date, offset, WIN, 2)  10.7 us
    unnamed x12, local copies, waits for them, and re-layouts  7.26 us
    another operation x2, other arithmetic  6.74 us
    add x1, other arithmetic, per_device(): real_sec * real_sec + imag_sec * imag_sec  5.12 us
    add x1, local copies, waits for them, and re-layouts, per_device(): real_sec * real_sec + imag_sec * imag_sec  4.82 us
  transfers between devices with their start and end apart: 1, of which 0 were waited for; matrix products, arithmetic and copies ran while one was open for 28% of the time, Pallas kernels for 0%

commit v1 on v0

v1 whole, which is shorter than its diff:
```python
import functools
import math

import jax
import jax.numpy as jnp
from jax import lax
from jax.experimental import pallas as pl
from jax.experimental.pallas import tpu as pltpu
from jax.sharding import PartitionSpec as P

TAPS = 8
LEAD = TAPS // 2 - 1
BLK = 128
WIN = 192
LOOK_AZ = 4
LOOK_RG = 16
HALF = 64
EPSILON = 1e-06
MESH = pl.DeviceIdType.MESH
SIN_TERMS = (4.442882919124343, -7.308245686509025, 3.6063542184321515, -0.8461116503693629, 0.10982451641673696)
COS_TERMS = (1.414213496255228, -6.978850948563791, 5.739460376906791, -1.8835579059844396, 0.3106880275224321)


def poly(terms, x):
    total = jnp.full_like(x, terms[-1])
    for term in terms[-2::-1]:
        total = total * x + term
    return total


def sincos_turns(turns):
    rest = turns - jnp.round(turns)
    square = rest * rest
    sine = rest * poly(SIN_TERMS, square)
    cosine = poly(COS_TERMS, square)
    return sine * cosine, 1.0 - sine * sine


def tap_weights(fraction):
    step = lax.broadcasted_iota(jnp.int32, (TAPS, fraction.shape[1]), 0) - LEAD
    spacing = step.astype(jnp.float32) - fraction
    angle = math.pi * spacing
    sine, _ = sincos_turns(spacing * 0.5)
    sinc = jnp.where(spacing == 0.0, 1.0, sine / jnp.where(spacing == 0.0, 1.0, angle))
    _, cosine = sincos_turns(spacing * 0.125)
    return sinc * (0.5 + 0.5 * cosine)


def tap_matrix(first, weights, cells):
    cell = lax.broadcasted_iota(jnp.int32, (cells, first.shape[1]), 0) - first
    total = jnp.zeros(cell.shape, jnp.float32)
    for k in range(TAPS):
        total = jnp.where(cell == k, weights[k : k + 1], total)
    return total.astype(jnp.bfloat16)


def slab_sum(values):
    rows = values.shape[0] // LOOK_AZ
    total = values[:rows]
    for b in range(1, LOOK_AZ):
        total = total + values[b * rows : (b + 1) * rows]
    return total


def looked(values, gather):
    high = values.astype(jnp.bfloat16)
    low = (values - high.astype(jnp.float32)).astype(jnp.bfloat16)
    return jnp.dot(jnp.concatenate([high, low], axis=1), gather, preferred_element_type=jnp.float32)


def kernel(
    parties,
    x_hbm, master_ref, rate_ref, center_ref, row_pos, row_frac, col_pos, col_frac, col_band,
    ifg_ref, stack_ref,
    x0, xs, weights, own_rc, rc, mg, res, times, place, acc, acc_sec, chunks, parts, totals,
    in_sems, rc_s, rc_r, m_s, m_r, p_s, p_r, t_s, t_r,
):
    me = lax.axis_index("date")
    lines_in = x0.shape[1]
    tiles_in = xs.shape[0] // 2
    last_half = xs.shape[0] - 3
    blocks = col_pos.shape[1] // BLK
    rows_out = row_pos.shape[1]
    looks_out = rows_out // LOOK_AZ
    per_tile = BLK * LOOK_RG // BLK

    fetch0 = pltpu.make_async_copy(x_hbm.at[0], x0, in_sems.at[0])
    fetch0.start()

    def tile_copy(t):
        lanes = pl.ds(pl.multiple_of(t * BLK, BLK), BLK)
        return pltpu.make_async_copy(x_hbm.at[0, :, :, lanes], xs.at[2 * t], in_sems.at[t + 1])

    def tile_start(t, _):
        tile_copy(t).start()
        return 0

    def tile_wait(t, _):
        tile_copy(t).wait()
        return 0

    lax.fori_loop(0, tiles_in, tile_start, 0)

    barrier = pltpu.get_barrier_semaphore()

    def greet(s, _):
        pl.semaphore_signal(barrier, inc=1, device_id={"date": lax.rem(me + s, parties)}, device_id_type=MESH)
        return 0

    lax.fori_loop(1, parties, greet, 0)

    own_rc[...] = jnp.zeros_like(own_rc)
    own_rc[0:1, :] = rate_ref[...] * (0.5 / math.pi)
    own_rc[1:2, :] = center_ref[...]
    rc[pl.ds(me, 1)] = own_rc[...][None]
    to = lax.broadcasted_iota(jnp.int32, (rows_out, rows_out), 0)
    source = lax.broadcasted_iota(jnp.int32, (rows_out, rows_out), 1)
    order = jnp.where(source == LOOK_AZ * (to % looks_out) + to // looks_out, 1.0, 0.0).astype(jnp.bfloat16)
    for p in range(2):
        mg[pl.ds(me, 1), p] = jnp.dot(order, master_ref[p], preferred_element_type=jnp.float32).astype(jnp.bfloat16)[None]

    pl.semaphore_wait(barrier, parties - 1)

    def rc_copy(slot, peer):
        return pltpu.make_async_remote_copy(
            src_ref=own_rc, dst_ref=rc.at[slot], send_sem=rc_s.at[peer], recv_sem=rc_r.at[slot],
            device_id={"date": peer}, device_id_type=MESH)

    def rc_send(s, _):
        rc_copy(me, lax.rem(me + s, parties)).start()
        return 0

    lax.fori_loop(1, parties, rc_send, 0)

    deep = parties // 4
    my_z, my_y, my_c = me // 4, (me // 2) % 2, me % 2
    across = my_z * 4 + (1 - my_y) * 2 + my_c
    twin = my_z * 4 + my_y * 2 + (1 - my_c)

    def m_copy(slot, peer, kind, tag):
        return pltpu.make_async_remote_copy(
            src_ref=mg.at[slot], dst_ref=mg.at[slot], send_sem=m_s.at[kind, tag], recv_sem=m_r.at[slot],
            device_id={"date": peer}, device_id_type=MESH)

    def z_index(s):
        return lax.rem(my_z + s, deep) * 4

    def z_send(s, _):
        peer = z_index(s) + my_y * 2 + my_c
        m_copy(me, peer, 0, peer).start()
        return 0

    m_copy(me, across, 1, me).start()
    lax.fori_loop(1, deep, z_send, 0)
    m_copy(me, twin, 2, me).start()

    def z_pass(s, _):
        slot = z_index(s) + my_y * 2 + my_c
        m_copy(slot, slot, 0, slot).wait_recv()
        m_copy(slot, across, 1, slot).start()
        m_copy(slot, twin, 2, slot).start()
        return 0

    def y_pass(s, _):
        slot = z_index(s) + (1 - my_y) * 2 + my_c
        m_copy(slot, across, 1, slot).wait_recv()
        m_copy(slot, twin, 2, slot).start()
        return 0

    def twin_wait(s, _):
        for y in range(2):
            slot = z_index(s) + y * 2 + (1 - my_c)
            m_copy(slot, twin, 2, slot).wait_recv()
        return 0

    weights[...] = tap_weights(col_frac[...])
    row_taps = tap_matrix(row_pos[...] - LEAD, tap_weights(row_frac[...]), lines_in)
    row_taps = lax.dot_general(
        order, row_taps, (((1,), (1,)), ((), ())), preferred_element_type=jnp.float32
    ).astype(jnp.bfloat16)
    when = (row_pos[...].astype(jnp.float32) + row_frac[...]) / lines_in
    times[...] = jnp.transpose(jnp.broadcast_to(when, (BLK, rows_out)))
    for b in range(LOOK_AZ):
        place[b * looks_out : (b + 1) * looks_out, :] = times[pl.ds(b, looks_out, stride=LOOK_AZ), :]
    lane = lax.broadcasted_iota(jnp.int32, (2 * BLK, BLK), 0) % BLK
    out_lane = lax.broadcasted_iota(jnp.int32, (2 * BLK, BLK), 1)
    gather = jnp.where(lane // LOOK_RG == out_lane, 1.0, 0.0).astype(jnp.bfloat16)
    acc[...] = jnp.zeros_like(acc)
    acc_sec[...] = jnp.zeros_like(acc_sec)

    fetch0.wait()
    lax.fori_loop(0, tiles_in, tile_wait, 0)
    for t in range(tiles_in):
        xs[2 * t + 1] = x0[:, :, t * BLK + HALF : (t + 1) * BLK + HALF]

    def rc_wait(s, _):
        slot = lax.rem(me + s, parties)
        rc_copy(slot, slot).wait_recv()
        return 0

    lax.fori_loop(1, parties, rc_wait, 0)

    line_time = lax.broadcasted_iota(jnp.int32, (lines_in, BLK), 0).astype(jnp.float32) / lines_in

    def resample(b, _):
        half = lax.min(lax.div(col_band[0, b], HALF), last_half)
        window = jnp.concatenate([xs[half], xs[half + 2]], axis=2).reshape(2 * lines_in, 2 * BLK)
        columns = pl.ds(pl.multiple_of(b * BLK, BLK), BLK)
        taps = tap_matrix(col_pos[:, columns] - (LEAD + HALF * half), weights[:, columns], 2 * BLK)
        ranged = jnp.dot(window, taps, preferred_element_type=jnp.float32)
        rate, center = rc[b, 0:1, :], rc[b, 1:2, :]
        offset = line_time - center
        sine, cosine = sincos_turns(rate * offset * offset)
        real, imag = ranged[:lines_in], ranged[lines_in:]
        deramped = jnp.concatenate(
            [(real * cosine + imag * sine).astype(jnp.bfloat16), (imag * cosine - real * sine).astype(jnp.bfloat16)],
            axis=1)
        moved = jnp.dot(row_taps, deramped, preferred_element_type=jnp.float32)
        offset = place[...] - center
        sine, cosine = sincos_turns(rate * offset * offset)
        real, imag = moved[:, :BLK], moved[:, BLK:]
        real, imag = (
            (real * cosine - imag * sine).astype(jnp.bfloat16),
            (real * sine + imag * cosine).astype(jnp.bfloat16),
        )
        res[b, 0] = real
        res[b, 1] = imag
        real, imag = real.astype(jnp.float32), imag.astype(jnp.float32)
        sums = looked(slab_sum(real * real + imag * imag), gather)
        acc_sec[b // per_tile] += pltpu.roll(sums, (b % per_tile) * (BLK // LOOK_RG), 1)
        return 0

    cut = blocks // 2
    lax.fori_loop(0, cut, resample, 0)
    lax.fori_loop(1, deep, z_pass, 0)
    lax.fori_loop(cut, blocks, resample, 0)
    lax.fori_loop(0, deep, y_pass, 0)

    per_slab = looks_out // 2
    scale = 1.0 / (LOOK_AZ * LOOK_RG)
    for d in range(parties):
        chunks[d] = acc_sec[d // per_slab, 2 * (d % per_slab) : 2 * (d % per_slab) + 2, :]

    def p_copy(chunk, slot, peer):
        return pltpu.make_async_remote_copy(
            src_ref=chunks.at[chunk], dst_ref=parts.at[slot], send_sem=p_s.at[peer], recv_sem=p_r.at[slot],
            device_id={"date": peer}, device_id_type=MESH)

    def p_send(s, _):
        peer = lax.rem(me + s, parties)
        p_copy(peer, me, peer).start()
        return 0

    lax.fori_loop(1, parties, p_send, 0)
    parts[pl.ds(me, 1)] = chunks[pl.ds(me, 1)]

    lax.fori_loop(0, deep, twin_wait, 0)

    def combine(b, _):
        m0, m1 = mg[b, 0].astype(jnp.float32), mg[b, 1].astype(jnp.float32)
        r0, r1 = res[b, 0].astype(jnp.float32), res[b, 1].astype(jnp.float32)
        rows = jnp.concatenate(
            [slab_sum(m0 * r0 + m1 * r1), slab_sum(m1 * r0 - m0 * r1), slab_sum(m0 * m0 + m1 * m1)], axis=0)
        sums = looked(rows, gather)
        acc[b // per_tile] += pltpu.roll(sums, (b % per_tile) * (BLK // LOOK_RG), 1)
        return 0

    lax.fori_loop(0, blocks // 2, combine, 0)

    def p_wait(s, _):
        slot = lax.rem(me + s, parties)
        p_copy(slot, slot, slot).wait_recv()
        return 0

    lax.fori_loop(1, parties, p_wait, 0)
    totals[pl.ds(me, 1)] = (jnp.sum(parts[...], axis=0) * (scale / parties))[None]

    def t_copy(slot, peer):
        return pltpu.make_async_remote_copy(
            src_ref=totals.at[slot], dst_ref=totals.at[slot], send_sem=t_s.at[peer], recv_sem=t_r.at[slot],
            device_id={"date": peer}, device_id_type=MESH)

    def t_send(s, _):
        t_copy(me, lax.rem(me + s, parties)).start()
        return 0

    lax.fori_loop(1, parties, t_send, 0)
    lax.fori_loop(blocks // 2, blocks, combine, 0)

    lane_tile = min(BLK, ifg_ref.shape[2])
    for t in range(ifg_ref.shape[2] // lane_tile):
        lanes = slice(t * lane_tile, (t + 1) * lane_tile)
        real, imag, ref = (acc[t, q * looks_out : (q + 1) * looks_out, :] * scale for q in range(3))
        normalizer = 1.0 / jnp.sqrt(ref * (acc_sec[t] * scale) + EPSILON)
        ifg_ref[0, :, lanes] = real * normalizer
        ifg_ref[1, :, lanes] = imag * normalizer

    def t_wait(s, _):
        slot = lax.rem(me + s, parties)
        t_copy(slot, slot).wait_recv()
        return 0

    lax.fori_loop(1, parties, t_wait, 0)
    for d in range(parties):
        stack_ref[2 * (d % per_slab) : 2 * (d % per_slab) + 2, (d // per_slab) * BLK : (d // per_slab + 1) * BLK] = totals[d]

    def sent(s, _):
        peer = lax.rem(me + s, parties)
        rc_copy(me, peer).wait_send()
        p_copy(peer, me, peer).wait_send()
        t_copy(me, peer).wait_send()
        return 0

    lax.fori_loop(1, parties, sent, 0)

    def z_sent(s, _):
        peer = z_index(s) + my_y * 2 + my_c
        m_copy(me, peer, 0, peer).wait_send()
        return 0

    def forward_sent(s, _):
        near = z_index(s) + my_y * 2 + my_c
        far = z_index(s) + (1 - my_y) * 2 + my_c
        m_copy(near, across, 1, near).wait_send()
        m_copy(near, twin, 2, near).wait_send()
        m_copy(far, twin, 2, far).wait_send()
        return 0

    lax.fori_loop(1, deep, z_sent, 0)
    lax.fori_loop(0, deep, forward_sent, 0)


def per_device(
    parties, x, master, rate, center, row_pos, row_frac, row_band, col_pos, col_frac, col_band,
):
    lines_in, cells = x.shape[2], x.shape[3]
    samples = col_pos.shape[1]
    rows_out = row_pos.shape[1]
    blocks = samples // BLK
    looks_out, look_lanes = rows_out // LOOK_AZ, samples // LOOK_RG
    tiles = -(-look_lanes // BLK)
    tiles_in = (cells - HALF) // BLK
    vmem = pl.BlockSpec(memory_space=pltpu.VMEM)
    dma = pltpu.SemaphoreType.DMA
    f32, bf16 = jnp.float32, jnp.bfloat16
    ifg, stack = pl.pallas_call(
        functools.partial(kernel, parties),
        out_shape=(
            jax.ShapeDtypeStruct((2, looks_out, look_lanes), f32),
            jax.ShapeDtypeStruct((looks_out, look_lanes), f32),
        ),
        in_specs=[pl.BlockSpec(memory_space=pl.ANY)] + [vmem] * 7 + [pl.BlockSpec(memory_space=pltpu.SMEM)],
        out_specs=(vmem, vmem),
        scratch_shapes=[
            pltpu.VMEM((2, lines_in, cells), bf16),
            pltpu.VMEM((2 * tiles_in, 2, lines_in, BLK), bf16),
            pltpu.VMEM((TAPS, samples), f32),
            pltpu.VMEM((8, BLK), f32),
            pltpu.VMEM((parties, 8, BLK), f32),
            pltpu.VMEM((parties, 2, rows_out, BLK), bf16),
            pltpu.VMEM((blocks, 2, rows_out, BLK), bf16),
            pltpu.VMEM((rows_out, BLK), f32),
            pltpu.VMEM((rows_out, BLK), f32),
            pltpu.VMEM((tiles, 3 * looks_out, BLK), f32),
            pltpu.VMEM((tiles, looks_out, BLK), f32),
            pltpu.VMEM((parties, 2, BLK), f32),
            pltpu.VMEM((parties, 2, BLK), f32),
            pltpu.VMEM((parties, 2, BLK), f32),
            dma((tiles_in + 1,)),
            dma((parties,)), dma((parties,)),
            dma((3, parties)), dma((parties,)),
            dma((parties,)), dma((parties,)),
            dma((parties,)), dma((parties,)),
        ],
        compiler_params=pltpu.CompilerParams(
            collective_id=0, has_side_effects=True, vmem_limit_bytes=48 * 1024 * 1024
        ),
        cost_estimate=pl.CostEstimate(flops=6 * 10**8, bytes_accessed=4 * 10**6, transcendentals=0),
        name="coregister",
    )(x, master, rate[None], center[None], row_pos, row_frac, col_pos, col_frac, col_band)
    return ifg[None], stack


def solution(mesh):
    placed = (
        P(("parts", "date"), None, None, None),
        P(None, "parts", "date"),
        P("date"),
        P("date"),
        P(("parts", "date"), None),
        P(("parts", "date"), None),
        P(("parts", "date"), None),
        P(("parts", "date"), None),
        P(("parts", "date"), None),
        P(("parts", "date"), None),
    )
    return jax.shard_map(
        functools.partial(per_device, mesh.shape["date"]),
        mesh=mesh,
        in_specs=placed,
        out_specs=(P(("parts", "date"), None, None, None), P("parts", None)),
        check_vma=False,
    )
```

time: 182 us -> 43.3 us (0.24)
  blocking collectives: 99.8 us -> 0 us
  Pallas kernels: 0 us -> 34.2 us
  other arithmetic: 33.2 us -> 0 us
  local copies, waits for them, and re-layouts: 30.8 us -> 8.16 us
  between operations: 14.8 us -> 0.66 us
  matrix products: 1.87 us -> 0 us
    psum x1 -> x0, blocking collectives: 59.2 us -> none  [per_device(): stack_power = lax.psum(sec_power, 'date') / lax.axis_size('date')]
    all_gather x2 -> x0, blocking collectives: 40.6 us -> none  [the longest x1 23.2 us: per_device(): lax.all_gather(deskew_angular_slope, 'date', axis=0, tiled=True)]
    pallas_call x0 -> x1, Pallas kernels: none -> 34.2 us  [per_device(): pl.pallas_call(functools.partial(kernel, parties), out_shape=(jax.ShapeDt...]
    reduce_sum x6 -> x0, other arithmetic: 12.1 us -> none  [the longest x1 4.38 us: per_device(): term_stack.reshape(3, term_stack.shape[1] // LOOK_AZ, LOOK_AZ, span_width)]
    gather x2 -> x0, local copies, waits for them, and re-layouts: 10.7 us -> none  [range_turn(): lax.dynamic_slice_in_dim(second_date, offset, WIN, 2)]
    add x2 -> x0, other arithmetic: 6.94 us -> none  [the longest x1 5.12 us: per_device(): real_sec * real_sec + imag_sec * imag_sec]
    another operation x2 -> x0, other arithmetic: 6.74 us -> none
    add x3 -> x0, local copies, waits for them, and re-layouts: 6.2 us -> none  [the longest x1 4.82 us: per_device(): real_sec * real_sec + imag_sec * imag_sec]
  transfers between devices with their start and end apart: 1 -> 0, of which waited for: 0 -> 0; matrix products, arithmetic and copies ran while one was open for 28% -> 0% of each run, Pallas kernels for 0% -> 0%
where the time goes in v1:
time: 43.3 us; the launch traced here: 43 us
  Pallas kernels  34.2 us (79%)
  local copies, waits for them, and re-layouts  8.16 us (19%)
  between operations  0.66 us (2%)
    pallas_call x1, Pallas kernels, per_device(): pl.pallas_call(functools.partial(kernel, parties), out_shape=(jax.ShapeDt...  34.2 us
    unnamed x20, local copies, waits for them, and re-layouts  8.16 us

profile of v1, /device:TPU:0, one launch (start us, length us, event | category | flops | bytes accessed | tf_op | source)
XLA Modules:
  0.0 43.0 jit_solution(86338216315938536)
XLA Ops:
  0.6 0.0 copy-start
  0.6 1.4 %copy-done = bf16[1,2,192,2112]{3,2,1,0:T(8,128)(2,1)S(1)} copy-done((bf16[1,2,192,2112]{3,2,1,0:T(8,128)(2,1)S(1)}, bf16[1,2,192,2112]{3,2,1,0:T(8,128)(2,1)}, u32[]{:S(2)}) %copy-start) | copy-done | bytes 1622040
  2.1 0.0 copy-start.1
  2.1 0.8 %copy-done.1 = bf16[2,128,128]{2,1,0:T(8,128)(2,1)S(1)} copy-done((bf16[2,128,128]{2,1,0:T(8,128)(2,1)S(1)}, bf16[2,128,128]{2,1,0:T(8,128)(2,1)}, u32[]{:S(2)}) %copy-start.1) | copy-done | bytes 65560
  2.9 0.0 copy-start.2
  2.9 0.7 %copy-done.2 = s32[1,2048]{1,0:T(1,128)S(1)} copy-done((s32[1,2048]{1,0:T(1,128)S(1)}, s32[1,2048]{1,0:T(1,128)}, u32[]{:S(2)}) %copy-start.2) | copy-done | bytes 8216
  3.6 0.0 copy-start.3
  3.6 0.7 %copy-done.3 = f32[1,2048]{1,0:T(1,128)S(1)} copy-done((f32[1,2048]{1,0:T(1,128)S(1)}, f32[1,2048]{1,0:T(1,128)}, u32[]{:S(2)}) %copy-start.3) | copy-done | bytes 8216
  4.3 0.0 copy-start.4
  4.3 0.7 %copy-done.4 = f32[128]{0:T(128)S(1)} copy-done((f32[128]{0:T(128)S(1)}, f32[128]{0:T(128)}, u32[]{:S(2)}) %copy-start.4) | copy-done | bytes 536
  5.0 0.0 copy-start.5
  5.0 0.7 %copy-done.5 = f32[128]{0:T(128)S(1)} copy-done((f32[128]{0:T(128)S(1)}, f32[128]{0:T(128)}, u32[]{:S(2)}) %copy-start.5) | copy-done | bytes 536
  5.6 0.0 copy-start.6
  5.6 0.7 %copy-done.6 = s32[1,128]{1,0:T(1,128)S(1)} copy-done((s32[1,128]{1,0:T(1,128)S(1)}, s32[1,128]{1,0:T(1,128)}, u32[]{:S(2)}) %copy-start.6) | copy-done | bytes 536
  6.3 0.0 copy-start.7
  6.3 0.7 %copy-done.7 = f32[1,128]{1,0:T(1,128)S(1)} copy-done((f32[1,128]{1,0:T(1,128)S(1)}, f32[1,128]{1,0:T(1,128)}, u32[]{:S(2)}) %copy-start.7) | copy-done | bytes 536
  6.9 0.0 copy-start.8
  6.9 0.7 %copy-done.8 = s32[1,16]{1,0:T(1,128)S(1)} copy-done((s32[1,16]{1,0:T(1,128)S(1)}, s32[1,16]{1,0:T(1,128)}, u32[]{:S(2)}) %copy-start.8) | copy-done | bytes 88
  7.6 34.2 %coregister.1 = (f32[2,32,128]{2,1,0:T(8,128)S(1)}, f32[32,128]{1,0:T(8,128)S(1)}) custom-call(bf16[1,2,192,2112]{3,2,1,0:T(8,128)(2,1)S(1)} %copy-done, bf16[2,128,128]{2,1,0:T(8,128)(2,1)S(1)} %copy-done.1, f32[1,128]{1,0:T(1,128)S(1)} %bitcast.4, f32[1,128]{1,0:T(1,128)S(1)} %bitcast.5, s32[1,128]{1,0:T(1,128)S(1)} %copy-done.6, f32[1,128]{1,0:T(1,128)S(1)} %copy-done.7, ...), custom_call_target="tpu_custom_call" | custom-call | flops 600000000 | bytes 4000000 | tf_op jit(solution)/shard_map/coregister/pallas_call | solution.py:346
  41.8 0.6 %copy.13 = f32[1,2,32,128]{3,2,1,0:T(8,128)} copy(f32[1,2,32,128]{3,2,1,0:T(8,128)S(1)} %bitcast.3) | data formatting | bytes 65536
  42.4 0.6 %copy.14 = f32[32,128]{1,0:T(8,128)} copy(f32[32,128]{1,0:T(8,128)S(1)} %get-tuple-element.9) | data formatting | bytes 32768
Async XLA Ops:
  0.6 1.4 %copy-start = (bf16[1,2,192,2112]{3,2,1,0:T(8,128)(2,1)S(1)}, bf16[1,2,192,2112]{3,2,1,0:T(8,128)(2,1)}, u32[]{:S(2)}) copy-start(bf16[1,2,192,2112]{3,2,1,0:T(8,128)(2,1)} %x_hbm.1) | copy-start | bytes 4866052
  2.1 0.8 %copy-start.1 = (bf16[2,128,128]{2,1,0:T(8,128)(2,1)S(1)}, bf16[2,128,128]{2,1,0:T(8,128)(2,1)}, u32[]{:S(2)}) copy-start(bf16[2,128,128]{2,1,0:T(8,128)(2,1)} %master_ref.1) | copy-start | bytes 196612
  2.9 0.7 %copy-start.2 = (s32[1,2048]{1,0:T(1,128)S(1)}, s32[1,2048]{1,0:T(1,128)}, u32[]{:S(2)}) copy-start(s32[1,2048]{1,0:T(1,128)} %col_pos.1) | copy-start | bytes 24580
  3.6 0.7 %copy-start.3 = (f32[1,2048]{1,0:T(1,128)S(1)}, f32[1,2048]{1,0:T(1,128)}, u32[]{:S(2)}) copy-start(f32[1,2048]{1,0:T(1,128)} %col_frac.1) | copy-start | bytes 24580
  4.3 0.7 %copy-start.4 = (f32[128]{0:T(128)S(1)}, f32[128]{0:T(128)}, u32[]{:S(2)}) copy-start(f32[128]{0:T(128)} %param.12) | copy-start | bytes 1540
  5.0 0.7 %copy-start.5 = (f32[128]{0:T(128)S(1)}, f32[128]{0:T(128)}, u32[]{:S(2)}) copy-start(f32[128]{0:T(128)} %param.13) | copy-start | bytes 1540
  5.6 0.7 %copy-start.6 = (s32[1,128]{1,0:T(1,128)S(1)}, s32[1,128]{1,0:T(1,128)}, u32[]{:S(2)}) copy-start(s32[1,128]{1,0:T(1,128)} %row_pos.1) | copy-start | bytes 1540
  6.3 0.7 %copy-start.7 = (f32[1,128]{1,0:T(1,128)S(1)}, f32[1,128]{1,0:T(1,128)}, u32[]{:S(2)}) copy-start(f32[1,128]{1,0:T(1,128)} %row_frac.1) | copy-start | bytes 1540
  6.9 0.7 %copy-start.8 = (s32[1,16]{1,0:T(1,128)S(1)}, s32[1,16]{1,0:T(1,128)}, u32[]{:S(2)}) copy-start(s32[1,16]{1,0:T(1,128)} %col_band.1) | copy-start | bytes 196

commit v2 on v1

--- a/solution.py
+++ b/solution.py
@@ -70,10 +70,11 @@
 
 def kernel(
     parties,
-    x_hbm, master_ref, rate_ref, center_ref, row_pos, row_frac, col_pos, col_frac, col_band,
+    x_hbm, master_hbm, rate_hbm, center_hbm, row_pos_hbm, row_frac_hbm, col_pos_hbm, col_frac_hbm, col_band_hbm,
     ifg_ref, stack_ref,
+    master_ref, rate_ref, center_ref, row_pos, row_frac, col_pos, col_frac, col_band,
     x0, xs, weights, own_rc, rc, mg, res, times, place, acc, acc_sec, chunks, parts, totals,
-    in_sems, rc_s, rc_r, m_s, m_r, p_s, p_r, t_s, t_r,
+    small_sems, in_sems, rc_s, rc_r, m_s, m_r, p_s, p_r, t_s, t_r,
 ):
     me = lax.axis_index("date")
     lines_in = x0.shape[1]
@@ -84,6 +85,14 @@
     looks_out = rows_out // LOOK_AZ
     per_tile = BLK * LOOK_RG // BLK
 
+    small = [
+        pltpu.make_async_copy(source, target, small_sems.at[i])
+        for i, (source, target) in enumerate((
+            (master_hbm, master_ref), (rate_hbm, rate_ref), (center_hbm, center_ref), (col_frac_hbm, col_frac),
+            (row_pos_hbm, row_pos), (row_frac_hbm, row_frac), (col_pos_hbm, col_pos), (col_band_hbm, col_band)))
+    ]
+    for copy in small:
+        copy.start()
     fetch0 = pltpu.make_async_copy(x_hbm.at[0], x0, in_sems.at[0])
     fetch0.start()
 
@@ -108,6 +117,9 @@
         return 0
 
     lax.fori_loop(1, parties, greet, 0)
+
+    for copy in small[:3]:
+        copy.wait()
 
     own_rc[...] = jnp.zeros_like(own_rc)
     own_rc[0:1, :] = rate_ref[...] * (0.5 / math.pi)
@@ -172,6 +184,9 @@
             slot = z_index(s) + y * 2 + (1 - my_c)
             m_copy(slot, twin, 2, slot).wait_recv()
         return 0
+
+    for copy in small[3:]:
+        copy.wait()
 
     weights[...] = tap_weights(col_frac[...])
     row_taps = tap_matrix(row_pos[...] - LEAD, tap_weights(row_frac[...]), lines_in)
@@ -349,9 +364,17 @@
             jax.ShapeDtypeStruct((2, looks_out, look_lanes), f32),
             jax.ShapeDtypeStruct((looks_out, look_lanes), f32),
         ),
-        in_specs=[pl.BlockSpec(memory_space=pl.ANY)] + [vmem] * 7 + [pl.BlockSpec(memory_space=pltpu.SMEM)],
+        in_specs=[pl.BlockSpec(memory_space=pl.ANY)] * 9,
         out_specs=(vmem, vmem),
         scratch_shapes=[
+            pltpu.VMEM(master.shape, bf16),
+            pltpu.VMEM((1, BLK), f32),
+            pltpu.VMEM((1, BLK), f32),
+            pltpu.VMEM(row_pos.shape, jnp.int32),
+            pltpu.VMEM(row_frac.shape, f32),
+            pltpu.VMEM(col_pos.shape, jnp.int32),
+            pltpu.VMEM(col_frac.shape, f32),
+            pltpu.SMEM(col_band.shape, jnp.int32),
             pltpu.VMEM((2, lines_in, cells), bf16),
             pltpu.VMEM((2 * tiles_in, 2, lines_in, BLK), bf16),
             pltpu.VMEM((TAPS, samples), f32),
@@ -366,6 +389,7 @@
             pltpu.VMEM((parties, 2, BLK), f32),
             pltpu.VMEM((parties, 2, BLK), f32),
             pltpu.VMEM((parties, 2, BLK), f32),
+            dma((8,)),
             dma((tiles_in + 1,)),
             dma((parties,)), dma((parties,)),
             dma((3, parties)), dma((parties,)),
@@ -373,7 +397,7 @@
             dma((parties,)), dma((parties,)),
         ],
         compiler_params=pltpu.CompilerParams(
-            collective_id=0, has_side_effects=True, vmem_limit_bytes=48 * 1024 * 1024
+            collective_id=0, has_side_effects=True, vmem_limit_bytes=60 * 1024 * 1024
         ),
         cost_estimate=pl.CostEstimate(flops=6 * 10**8, bytes_accessed=4 * 10**6, transcendentals=0),
         name="coregister",

time: 43.3 us -> 37.4 us (0.86)
  local copies, waits for them, and re-layouts: 8.16 us -> 2.7 us
    unnamed x20 -> x2, local copies, waits for them, and re-layouts: 8.16 us -> 2.7 us
where the time goes in v2:
time: 37.4 us; the launch traced here: 37.2 us
  Pallas kernels  33.8 us (90%)
  local copies, waits for them, and re-layouts  2.7 us (7%)
  between operations  0.64 us (2%)
    pallas_call x1, Pallas kernels, per_device(): pl.pallas_call(functools.partial(kernel, parties), out_shape=(jax.ShapeDt...  33.8 us
    unnamed x2, local copies, waits for them, and re-layouts  2.7 us

profile of v2, /device:TPU:0, one launch (start us, length us, event | category | flops | bytes accessed | tf_op | source)
XLA Modules:
  0.0 37.2 jit_solution(9029019955128125989)
XLA Ops:
  0.6 33.8 %coregister.1 = (f32[2,32,128]{2,1,0:T(8,128)}, f32[32,128]{1,0:T(8,128)}) custom-call(bf16[1,2,192,2112]{3,2,1,0:T(8,128)(2,1)} %x_hbm.1, bf16[2,128,128]{2,1,0:T(8,128)(2,1)} %master_hbm.1, f32[1,128]{1,0:T(1,128)} %bitcast.4, f32[1,128]{1,0:T(1,128)} %bitcast.5, s32[1,128]{1,0:T(1,128)} %row_pos_hbm.1, f32[1,128]{1,0:T(1,128)} %row_frac_hbm.1, ...), custom_call_target="tpu_custom_call" | custom-call | flops 600000000 | bytes 4000000 | tf_op jit(solution)/shard_map/coregister/pallas_call | solution.py:361
  34.5 1.4 %copy.13 = f32[1,2,32,128]{3,2,1,0:T(8,128)} copy(f32[1,2,32,128]{3,2,1,0:T(8,128)} %bitcast.3) | data formatting | bytes 65536
  35.8 1.3 %copy.14 = f32[32,128]{1,0:T(8,128)} copy(f32[32,128]{1,0:T(8,128)} %get-tuple-element.9) | data formatting | bytes 32768

commit v3 on v2

--- a/solution.py
+++ b/solution.py
@@ -71,19 +71,26 @@
 def kernel(
     parties,
     x_hbm, master_hbm, rate_hbm, center_hbm, row_pos_hbm, row_frac_hbm, col_pos_hbm, col_frac_hbm, col_band_hbm,
-    ifg_ref, stack_ref,
+    out_ref,
     master_ref, rate_ref, center_ref, row_pos, row_frac, col_pos, col_frac, col_band,
-    x0, xs, weights, own_rc, rc, mg, res, times, place, acc, acc_sec, chunks, parts, totals,
-    small_sems, in_sems, rc_s, rc_r, m_s, m_r, p_s, p_r, t_s, t_r,
+    x0, xs, weights, own_rc, rc, mg, res, times, place, acc, sec, outgoing, powers,
+    small_sems, in_sems, rc_s, rc_r, m_s, m_r, p_s, p_r,
 ):
     me = lax.axis_index("date")
+    deep = parties // 4
+    my_z, my_y, my_c = me // 4, (me // 2) % 2, me % 2
+    across = my_z * 4 + (1 - my_y) * 2 + my_c
+    twin = my_z * 4 + my_y * 2 + (1 - my_c)
     lines_in = x0.shape[1]
     tiles_in = xs.shape[0] // 2
     last_half = xs.shape[0] - 3
     blocks = col_pos.shape[1] // BLK
     rows_out = row_pos.shape[1]
     looks_out = rows_out // LOOK_AZ
-    per_tile = BLK * LOOK_RG // BLK
+    shift = BLK // LOOK_RG
+    per_tile = BLK // shift
+    per_part = per_tile // 2
+    part_steps = per_part // 2
 
     small = [
         pltpu.make_async_copy(source, target, small_sems.at[i])
@@ -135,8 +142,14 @@
 
     def rc_copy(slot, peer):
         return pltpu.make_async_remote_copy(
-            src_ref=own_rc, dst_ref=rc.at[slot], send_sem=rc_s.at[peer], recv_sem=rc_r.at[slot],
+            src_ref=own_rc, dst_ref=rc.at[slot], send_sem=rc_s, recv_sem=rc_r,
             device_id={"date": peer}, device_id_type=MESH)
+
+    def rc_all():
+        every = rc.at[pl.ds(0, parties - 1)]
+        return pltpu.make_async_remote_copy(
+            src_ref=every, dst_ref=every, send_sem=rc_s, recv_sem=rc_r,
+            device_id={"date": twin}, device_id_type=MESH)
 
     def rc_send(s, _):
         rc_copy(me, lax.rem(me + s, parties)).start()
@@ -144,10 +157,6 @@
 
     lax.fori_loop(1, parties, rc_send, 0)
 
-    deep = parties // 4
-    my_z, my_y, my_c = me // 4, (me // 2) % 2, me % 2
-    across = my_z * 4 + (1 - my_y) * 2 + my_c
-    twin = my_z * 4 + my_y * 2 + (1 - my_c)
 
     def m_copy(slot, peer, kind, tag):
         return pltpu.make_async_remote_copy(
@@ -201,23 +210,18 @@
     out_lane = lax.broadcasted_iota(jnp.int32, (2 * BLK, BLK), 1)
     gather = jnp.where(lane // LOOK_RG == out_lane, 1.0, 0.0).astype(jnp.bfloat16)
     acc[...] = jnp.zeros_like(acc)
-    acc_sec[...] = jnp.zeros_like(acc_sec)
+    sec[...] = jnp.zeros_like(sec)
 
     fetch0.wait()
     lax.fori_loop(0, tiles_in, tile_wait, 0)
     for t in range(tiles_in):
         xs[2 * t + 1] = x0[:, :, t * BLK + HALF : (t + 1) * BLK + HALF]
 
-    def rc_wait(s, _):
-        slot = lax.rem(me + s, parties)
-        rc_copy(slot, slot).wait_recv()
-        return 0
-
-    lax.fori_loop(1, parties, rc_wait, 0)
+    rc_all().wait_recv()
 
     line_time = lax.broadcasted_iota(jnp.int32, (lines_in, BLK), 0).astype(jnp.float32) / lines_in
 
-    def resample(b, _):
+    def resample(b):
         half = lax.min(lax.div(col_band[0, b], HALF), last_half)
         window = jnp.concatenate([xs[half], xs[half + 2]], axis=2).reshape(2 * lines_in, 2 * BLK)
         columns = pl.ds(pl.multiple_of(b * BLK, BLK), BLK)
@@ -242,91 +246,87 @@
         res[b, 1] = imag
         real, imag = real.astype(jnp.float32), imag.astype(jnp.float32)
         sums = looked(slab_sum(real * real + imag * imag), gather)
-        acc_sec[b // per_tile] += pltpu.roll(sums, (b % per_tile) * (BLK // LOOK_RG), 1)
-        return 0
-
-    cut = blocks // 2
-    lax.fori_loop(0, cut, resample, 0)
-    lax.fori_loop(1, deep, z_pass, 0)
-    lax.fori_loop(cut, blocks, resample, 0)
-    lax.fori_loop(0, deep, y_pass, 0)
-
-    per_slab = looks_out // 2
-    scale = 1.0 / (LOOK_AZ * LOOK_RG)
-    for d in range(parties):
-        chunks[d] = acc_sec[d // per_slab, 2 * (d % per_slab) : 2 * (d % per_slab) + 2, :]
-
-    def p_copy(chunk, slot, peer):
+        sec[b // per_part] += pltpu.roll(sums, (b % per_part) * shift, 1)
+
+    def p_copy(part, peer):
         return pltpu.make_async_remote_copy(
-            src_ref=chunks.at[chunk], dst_ref=parts.at[slot], send_sem=p_s.at[peer], recv_sem=p_r.at[slot],
+            src_ref=outgoing.at[part], dst_ref=powers.at[part, me], send_sem=p_s.at[part], recv_sem=p_r.at[part],
             device_id={"date": peer}, device_id_type=MESH)
 
-    def p_send(s, _):
-        peer = lax.rem(me + s, parties)
-        p_copy(peer, me, peer).start()
-        return 0
-
-    lax.fori_loop(1, parties, p_send, 0)
-    parts[pl.ds(me, 1)] = chunks[pl.ds(me, 1)]
-
+    def p_all(part):
+        every = powers.at[part, pl.ds(0, parties - 1)]
+        return pltpu.make_async_remote_copy(
+            src_ref=every, dst_ref=every, send_sem=p_s.at[part], recv_sem=p_r.at[part],
+            device_id={"date": twin}, device_id_type=MESH)
+
+    def step(i, _):
+        resample(2 * i)
+        resample(2 * i + 1)
+
+        @pl.when(i == 1)
+        def _():
+            lax.fori_loop(1, deep, z_pass, 0)
+
+        @pl.when(i == 5)
+        def _():
+            lax.fori_loop(0, deep, y_pass, 0)
+
+        @pl.when(i % part_steps == part_steps - 1)
+        def _():
+            part = i // part_steps
+            here = sec[part]
+            packed = here[: looks_out // 2] + pltpu.roll(here[looks_out // 2 :], BLK // 2, 1)
+            packed = packed.astype(jnp.bfloat16)
+            outgoing[part] = packed
+            powers[part, pl.ds(me, 1)] = packed[None]
+
+            def p_send(s, _):
+                p_copy(part, lax.rem(me + s, parties)).start()
+                return 0
+
+            lax.fori_loop(1, parties, p_send, 0)
+
+        return 0
+
+    lax.fori_loop(0, blocks // 2, step, 0)
     lax.fori_loop(0, deep, twin_wait, 0)
 
-    def combine(b, _):
+    def combine(b):
         m0, m1 = mg[b, 0].astype(jnp.float32), mg[b, 1].astype(jnp.float32)
         r0, r1 = res[b, 0].astype(jnp.float32), res[b, 1].astype(jnp.float32)
         rows = jnp.concatenate(
             [slab_sum(m0 * r0 + m1 * r1), slab_sum(m1 * r0 - m0 * r1), slab_sum(m0 * m0 + m1 * m1)], axis=0)
         sums = looked(rows, gather)
-        acc[b // per_tile] += pltpu.roll(sums, (b % per_tile) * (BLK // LOOK_RG), 1)
-        return 0
-
-    lax.fori_loop(0, blocks // 2, combine, 0)
-
-    def p_wait(s, _):
-        slot = lax.rem(me + s, parties)
-        p_copy(slot, slot, slot).wait_recv()
-        return 0
-
-    lax.fori_loop(1, parties, p_wait, 0)
-    totals[pl.ds(me, 1)] = (jnp.sum(parts[...], axis=0) * (scale / parties))[None]
-
-    def t_copy(slot, peer):
-        return pltpu.make_async_remote_copy(
-            src_ref=totals.at[slot], dst_ref=totals.at[slot], send_sem=t_s.at[peer], recv_sem=t_r.at[slot],
-            device_id={"date": peer}, device_id_type=MESH)
-
-    def t_send(s, _):
-        t_copy(me, lax.rem(me + s, parties)).start()
-        return 0
-
-    lax.fori_loop(1, parties, t_send, 0)
-    lax.fori_loop(blocks // 2, blocks, combine, 0)
-
-    lane_tile = min(BLK, ifg_ref.shape[2])
-    for t in range(ifg_ref.shape[2] // lane_tile):
-        lanes = slice(t * lane_tile, (t + 1) * lane_tile)
+        acc[b // per_tile] += pltpu.roll(sums, (b % per_tile) * shift, 1)
+
+    def combine_step(i, _):
+        combine(2 * i)
+        combine(2 * i + 1)
+        return 0
+
+    lax.fori_loop(0, blocks // 2, combine_step, 0)
+
+    scale = 1.0 / (LOOK_AZ * LOOK_RG)
+    left = lax.broadcasted_iota(jnp.int32, (looks_out // 2, BLK), 1) < BLK // 2
+    for t in range(blocks // per_tile):
+        lanes = slice(t * BLK, (t + 1) * BLK)
         real, imag, ref = (acc[t, q * looks_out : (q + 1) * looks_out, :] * scale for q in range(3))
-        normalizer = 1.0 / jnp.sqrt(ref * (acc_sec[t] * scale) + EPSILON)
-        ifg_ref[0, :, lanes] = real * normalizer
-        ifg_ref[1, :, lanes] = imag * normalizer
-
-    def t_wait(s, _):
-        slot = lax.rem(me + s, parties)
-        t_copy(slot, slot).wait_recv()
-        return 0
-
-    lax.fori_loop(1, parties, t_wait, 0)
-    for d in range(parties):
-        stack_ref[2 * (d % per_slab) : 2 * (d % per_slab) + 2, (d // per_slab) * BLK : (d // per_slab + 1) * BLK] = totals[d]
-
-    def sent(s, _):
-        peer = lax.rem(me + s, parties)
-        rc_copy(me, peer).wait_send()
-        p_copy(peer, me, peer).wait_send()
-        t_copy(me, peer).wait_send()
-        return 0
-
-    lax.fori_loop(1, parties, sent, 0)
+        mine = (sec[2 * t] + pltpu.roll(sec[2 * t + 1], BLK // 2, 1)) * scale
+        normalizer = 1.0 / jnp.sqrt(ref * mine + EPSILON)
+        out_ref[0, :, lanes] = real * normalizer
+        out_ref[1, :, lanes] = imag * normalizer
+    for t in range(blocks // per_tile):
+        lanes = slice(t * BLK, (t + 1) * BLK)
+        p_all(2 * t).wait_recv()
+        p_all(2 * t + 1).wait_recv()
+        first, second = (
+            jnp.sum(powers[2 * t + q].astype(jnp.float32), axis=0) * (scale / parties) for q in range(2))
+        out_ref[2, : looks_out // 2, lanes] = jnp.where(left, first, pltpu.roll(second, BLK // 2, 1))
+        out_ref[2, looks_out // 2 :, lanes] = jnp.where(left, pltpu.roll(first, BLK // 2, 1), second)
+
+    rc_all().wait_send()
+    for part in range(blocks // per_part):
+        p_all(part).wait_send()
 
     def z_sent(s, _):
         peer = z_index(s) + my_y * 2 + my_c
@@ -358,14 +358,11 @@
     vmem = pl.BlockSpec(memory_space=pltpu.VMEM)
     dma = pltpu.SemaphoreType.DMA
     f32, bf16 = jnp.float32, jnp.bfloat16
-    ifg, stack = pl.pallas_call(
+    out = pl.pallas_call(
         functools.partial(kernel, parties),
-        out_shape=(
-            jax.ShapeDtypeStruct((2, looks_out, look_lanes), f32),
-            jax.ShapeDtypeStruct((looks_out, look_lanes), f32),
-        ),
+        out_shape=jax.ShapeDtypeStruct((3, looks_out, look_lanes), f32),
         in_specs=[pl.BlockSpec(memory_space=pl.ANY)] * 9,
-        out_specs=(vmem, vmem),
+        out_specs=vmem,
         scratch_shapes=[
             pltpu.VMEM(master.shape, bf16),
             pltpu.VMEM((1, BLK), f32),
@@ -385,16 +382,14 @@
             pltpu.VMEM((rows_out, BLK), f32),
             pltpu.VMEM((rows_out, BLK), f32),
             pltpu.VMEM((tiles, 3 * looks_out, BLK), f32),
-            pltpu.VMEM((tiles, looks_out, BLK), f32),
-            pltpu.VMEM((parties, 2, BLK), f32),
-            pltpu.VMEM((parties, 2, BLK), f32),
-            pltpu.VMEM((parties, 2, BLK), f32),
+            pltpu.VMEM((2 * tiles, looks_out, BLK), f32),
+            pltpu.VMEM((2 * tiles, looks_out // 2, BLK), bf16),
+            pltpu.VMEM((2 * tiles, parties, looks_out // 2, BLK), bf16),
             dma((8,)),
             dma((tiles_in + 1,)),
-            dma((parties,)), dma((parties,)),
+            dma, dma,
             dma((3, parties)), dma((parties,)),
-            dma((parties,)), dma((parties,)),
-            dma((parties,)), dma((parties,)),
+            dma((2 * tiles,)), dma((2 * tiles,)),
         ],
         compiler_params=pltpu.CompilerParams(
             collective_id=0, has_side_effects=True, vmem_limit_bytes=60 * 1024 * 1024
@@ -402,7 +397,7 @@
         cost_estimate=pl.CostEstimate(flops=6 * 10**8, bytes_accessed=4 * 10**6, transcendentals=0),
         name="coregister",
     )(x, master, rate[None], center[None], row_pos, row_frac, col_pos, col_frac, col_band)
-    return ifg[None], stack
+    return out[None, :2], out[2]
 
 
 def solution(mesh):

time: 37.4 us -> 32.3 us (0.86)
  Pallas kernels: 33.8 us -> 28.8 us
    pallas_call x1, Pallas kernels: 33.8 us -> 28.8 us  [per_device(): pl.pallas_call(functools.partial(kernel, parties), out_shape=jax.ShapeDty...]
    unnamed x2 -> x0, local copies, waits for them, and re-layouts: 2.7 us -> none
    broadcast_in_dim x0 -> x1, local copies, waits for them, and re-layouts: none -> 1.37 us  [per_device(): return (out[None, :2], out[2])]
    squeeze x0 -> x1, local copies, waits for them, and re-layouts: none -> 1.32 us  [per_device(): return (out[None, :2], out[2])]
where the time goes in v3:
time: 32.3 us; the launch traced here: 32.1 us
  Pallas kernels  28.8 us (89%)
  local copies, waits for them, and re-layouts  2.7 us (8%)
  between operations  0.64 us (2%)
    pallas_call x1, Pallas kernels, per_device(): pl.pallas_call(functools.partial(kernel, parties), out_shape=jax.ShapeDty...  28.8 us
    broadcast_in_dim x1, local copies, waits for them, and re-layouts, per_device(): return (out[None, :2], out[2])  1.37 us
    squeeze x1, local copies, waits for them, and re-layouts, per_device(): return (out[None, :2], out[2])  1.32 us

profile of v3, /device:TPU:0, one launch (start us, length us, event | category | flops | bytes accessed | tf_op | source)
XLA Modules:
  0.0 32.1 jit_solution(624919476037231096)
XLA Ops:
  0.6 28.8 %coregister.1 = f32[3,32,128]{2,1,0:T(8,128)} custom-call(bf16[1,2,192,2112]{3,2,1,0:T(8,128)(2,1)} %x_hbm.1, bf16[2,128,128]{2,1,0:T(8,128)(2,1)} %master_hbm.1, f32[1,128]{1,0:T(1,128)} %bitcast.6, f32[1,128]{1,0:T(1,128)} %bitcast.7, s32[1,128]{1,0:T(1,128)} %row_pos_hbm.1, f32[1,128]{1,0:T(1,128)} %row_frac_hbm.1, s32[1,2048]{1,0:T(1,128)} %col_pos_hbm.1, ...), custom_call_target="tpu_custom_call" | custom-call | flops 600000000 | bytes 4000000 | tf_op jit(solution)/shard_map/coregister/pallas_call | solution.py:361
  29.4 1.3 %slice_bitcast_fusion.1 = f32[32,128]{1,0:T(8,128)} fusion(f32[3,32,128]{2,1,0:T(8,128)} %coregister.1), kind=kLoop, calls=%fused_computation.1 | loop fusion | bytes 32768 | tf_op jit(solution)/shard_map/squeeze | solution.py:400
  30.7 1.4 %slice_bitcast_fusion = f32[1,2,32,128]{3,2,1,0:T(8,128)} fusion(f32[3,32,128]{2,1,0:T(8,128)} %coregister.1), kind=kLoop, calls=%fused_computation | loop fusion | bytes 65536 | tf_op jit(solution)/shard_map/broadcast_in_dim | solution.py:400

commit v4 on v3

--- a/solution.py
+++ b/solution.py
@@ -62,18 +62,27 @@
     return total
 
 
-def looked(values, gather):
+def halves(values):
     high = values.astype(jnp.bfloat16)
     low = (values - high.astype(jnp.float32)).astype(jnp.bfloat16)
-    return jnp.dot(jnp.concatenate([high, low], axis=1), gather, preferred_element_type=jnp.float32)
+    return jnp.concatenate([high, low], axis=1)
+
+
+def looked(rows, gather, shift):
+    count, height, width = rows.shape
+    sums = jnp.dot(rows.reshape(count * height, width), gather, preferred_element_type=jnp.float32)
+    total = sums[:height]
+    for b in range(1, count):
+        total = total + pltpu.roll(sums[b * height : (b + 1) * height], b * shift, 1)
+    return total
 
 
 def kernel(
     parties,
     x_hbm, master_hbm, rate_hbm, center_hbm, row_pos_hbm, row_frac_hbm, col_pos_hbm, col_frac_hbm, col_band_hbm,
-    out_ref,
+    ifg_ref, stack_ref,
     master_ref, rate_ref, center_ref, row_pos, row_frac, col_pos, col_frac, col_band,
-    x0, xs, weights, own_rc, rc, mg, res, times, place, acc, sec, outgoing, powers,
+    x0, xs, weights, own_rc, rc, mg, res, times, place, rows_all, sec_rows, sec, outgoing, powers,
     small_sems, in_sems, rc_s, rc_r, m_s, m_r, p_s, p_r,
 ):
     me = lax.axis_index("date")
@@ -90,7 +99,7 @@
     shift = BLK // LOOK_RG
     per_tile = BLK // shift
     per_part = per_tile // 2
-    part_steps = per_part // 2
+    part_steps = per_part // 4
 
     small = [
         pltpu.make_async_copy(source, target, small_sems.at[i])
@@ -188,11 +197,13 @@
         m_copy(slot, twin, 2, slot).start()
         return 0
 
-    def twin_wait(s, _):
-        for y in range(2):
+    def twin_wait(y):
+        def wait(s, _):
             slot = z_index(s) + y * 2 + (1 - my_c)
             m_copy(slot, twin, 2, slot).wait_recv()
-        return 0
+            return 0
+
+        lax.fori_loop(0, deep, wait, 0)
 
     for copy in small[3:]:
         copy.wait()
@@ -209,8 +220,6 @@
     lane = lax.broadcasted_iota(jnp.int32, (2 * BLK, BLK), 0) % BLK
     out_lane = lax.broadcasted_iota(jnp.int32, (2 * BLK, BLK), 1)
     gather = jnp.where(lane // LOOK_RG == out_lane, 1.0, 0.0).astype(jnp.bfloat16)
-    acc[...] = jnp.zeros_like(acc)
-    sec[...] = jnp.zeros_like(sec)
 
     fetch0.wait()
     lax.fori_loop(0, tiles_in, tile_wait, 0)
@@ -245,8 +254,7 @@
         res[b, 0] = real
         res[b, 1] = imag
         real, imag = real.astype(jnp.float32), imag.astype(jnp.float32)
-        sums = looked(slab_sum(real * real + imag * imag), gather)
-        sec[b // per_part] += pltpu.roll(sums, (b % per_part) * shift, 1)
+        sec_rows[b] = halves(slab_sum(real * real + imag * imag))
 
     def p_copy(part, peer):
         return pltpu.make_async_remote_copy(
@@ -260,21 +268,18 @@
             device_id={"date": twin}, device_id_type=MESH)
 
     def step(i, _):
-        resample(2 * i)
-        resample(2 * i + 1)
+        for q in range(4):
+            resample(4 * i + q)
 
         @pl.when(i == 1)
         def _():
             lax.fori_loop(1, deep, z_pass, 0)
 
-        @pl.when(i == 5)
-        def _():
-            lax.fori_loop(0, deep, y_pass, 0)
-
         @pl.when(i % part_steps == part_steps - 1)
         def _():
             part = i // part_steps
-            here = sec[part]
+            here = looked(sec_rows[pl.ds(part * per_part, per_part)], gather, shift)
+            sec[part] = here
             packed = here[: looks_out // 2] + pltpu.roll(here[looks_out // 2 :], BLK // 2, 1)
             packed = packed.astype(jnp.bfloat16)
             outgoing[part] = packed
@@ -288,41 +293,48 @@
 
         return 0
 
-    lax.fori_loop(0, blocks // 2, step, 0)
-    lax.fori_loop(0, deep, twin_wait, 0)
-
+    lax.fori_loop(0, blocks // 4, step, 0)
     def combine(b):
         m0, m1 = mg[b, 0].astype(jnp.float32), mg[b, 1].astype(jnp.float32)
         r0, r1 = res[b, 0].astype(jnp.float32), res[b, 1].astype(jnp.float32)
         rows = jnp.concatenate(
             [slab_sum(m0 * r0 + m1 * r1), slab_sum(m1 * r0 - m0 * r1), slab_sum(m0 * m0 + m1 * m1)], axis=0)
-        sums = looked(rows, gather)
-        acc[b // per_tile] += pltpu.roll(sums, (b % per_tile) * shift, 1)
-
-    def combine_step(i, _):
-        combine(2 * i)
-        combine(2 * i + 1)
-        return 0
-
-    lax.fori_loop(0, blocks // 2, combine_step, 0)
+        rows_all[b] = halves(rows)
+
+    def combine_some(y, c):
+        def combine_step(i, _):
+            combine(8 * i + 2 * y + c)
+            combine(8 * i + 4 + 2 * y + c)
+            return 0
+
+        lax.fori_loop(0, deep // 2, combine_step, 0)
+
+    combine_some(my_y, my_c)
+    twin_wait(my_y)
+    lax.fori_loop(0, deep, y_pass, 0)
+    combine_some(my_y, 1 - my_c)
+    combine_some(1 - my_y, my_c)
+    twin_wait(1 - my_y)
+    combine_some(1 - my_y, 1 - my_c)
 
     scale = 1.0 / (LOOK_AZ * LOOK_RG)
     left = lax.broadcasted_iota(jnp.int32, (looks_out // 2, BLK), 1) < BLK // 2
     for t in range(blocks // per_tile):
         lanes = slice(t * BLK, (t + 1) * BLK)
-        real, imag, ref = (acc[t, q * looks_out : (q + 1) * looks_out, :] * scale for q in range(3))
+        sums = looked(rows_all[t * per_tile : (t + 1) * per_tile], gather, shift) * scale
+        real, imag, ref = (sums[q * looks_out : (q + 1) * looks_out] for q in range(3))
         mine = (sec[2 * t] + pltpu.roll(sec[2 * t + 1], BLK // 2, 1)) * scale
         normalizer = 1.0 / jnp.sqrt(ref * mine + EPSILON)
-        out_ref[0, :, lanes] = real * normalizer
-        out_ref[1, :, lanes] = imag * normalizer
+        ifg_ref[0, :, lanes] = real * normalizer
+        ifg_ref[1, :, lanes] = imag * normalizer
     for t in range(blocks // per_tile):
         lanes = slice(t * BLK, (t + 1) * BLK)
         p_all(2 * t).wait_recv()
         p_all(2 * t + 1).wait_recv()
         first, second = (
             jnp.sum(powers[2 * t + q].astype(jnp.float32), axis=0) * (scale / parties) for q in range(2))
-        out_ref[2, : looks_out // 2, lanes] = jnp.where(left, first, pltpu.roll(second, BLK // 2, 1))
-        out_ref[2, looks_out // 2 :, lanes] = jnp.where(left, pltpu.roll(first, BLK // 2, 1), second)
+        stack_ref[: looks_out // 2, lanes] = jnp.where(left, first, pltpu.roll(second, BLK // 2, 1))
+        stack_ref[looks_out // 2 :, lanes] = jnp.where(left, pltpu.roll(first, BLK // 2, 1), second)
 
     rc_all().wait_send()
     for part in range(blocks // per_part):
@@ -358,11 +370,14 @@
     vmem = pl.BlockSpec(memory_space=pltpu.VMEM)
     dma = pltpu.SemaphoreType.DMA
     f32, bf16 = jnp.float32, jnp.bfloat16
-    out = pl.pallas_call(
+    ifg, stack = pl.pallas_call(
         functools.partial(kernel, parties),
-        out_shape=jax.ShapeDtypeStruct((3, looks_out, look_lanes), f32),
+        out_shape=(
+            jax.ShapeDtypeStruct((2, looks_out, look_lanes), f32),
+            jax.ShapeDtypeStruct((looks_out, look_lanes), f32),
+        ),
         in_specs=[pl.BlockSpec(memory_space=pl.ANY)] * 9,
-        out_specs=vmem,
+        out_specs=(vmem, vmem),
         scratch_shapes=[
             pltpu.VMEM(master.shape, bf16),
             pltpu.VMEM((1, BLK), f32),
@@ -381,7 +396,8 @@
             pltpu.VMEM((blocks, 2, rows_out, BLK), bf16),
             pltpu.VMEM((rows_out, BLK), f32),
             pltpu.VMEM((rows_out, BLK), f32),
-            pltpu.VMEM((tiles, 3 * looks_out, BLK), f32),
+            pltpu.VMEM((blocks, 3 * looks_out, 2 * BLK), bf16),
+            pltpu.VMEM((blocks, looks_out, 2 * BLK), bf16),
             pltpu.VMEM((2 * tiles, looks_out, BLK), f32),
             pltpu.VMEM((2 * tiles, looks_out // 2, BLK), bf16),
             pltpu.VMEM((2 * tiles, parties, looks_out // 2, BLK), bf16),
@@ -397,7 +413,7 @@
         cost_estimate=pl.CostEstimate(flops=6 * 10**8, bytes_accessed=4 * 10**6, transcendentals=0),
         name="coregister",
     )(x, master, rate[None], center[None], row_pos, row_frac, col_pos, col_frac, col_band)
-    return out[None, :2], out[2]
+    return ifg[None], stack
 
 
 def solution(mesh):

time: 32.3 us -> 28.4 us (0.88)
  the two profiles are of different devices: /device:TPU:0 before, /device:TPU:1 now
where the time goes in v4:
time: 28.4 us; the launch traced here: 28.2 us
  Pallas kernels  24.8 us (87%)
  local copies, waits for them, and re-layouts  2.7 us (10%)
  between operations  0.64 us (2%)
    pallas_call x1, Pallas kernels, per_device(): pl.pallas_call(functools.partial(kernel, parties), out_shape=(jax.ShapeDt...  24.8 us
    unnamed x2, local copies, waits for them, and re-layouts  2.7 us

profile of v4, /device:TPU:1, one launch (start us, length us, event | category | flops | bytes accessed | tf_op | source)
XLA Modules:
  0.0 28.2 jit_solution(7813938050415279410)
XLA Ops:
  0.6 24.8 %coregister.1 = (f32[2,32,128]{2,1,0:T(8,128)}, f32[32,128]{1,0:T(8,128)}) custom-call(bf16[1,2,192,2112]{3,2,1,0:T(8,128)(2,1)} %x_hbm.1, bf16[2,128,128]{2,1,0:T(8,128)(2,1)} %master_hbm.1, f32[1,128]{1,0:T(1,128)} %bitcast.4, f32[1,128]{1,0:T(1,128)} %bitcast.5, s32[1,128]{1,0:T(1,128)} %row_pos_hbm.1, f32[1,128]{1,0:T(1,128)} %row_frac_hbm.1, ...), custom_call_target="tpu_custom_call" | custom-call | flops 600000000 | bytes 4000000 | tf_op jit(solution)/shard_map/coregister/pallas_call | solution.py:373
  25.5 1.4 %copy.13 = f32[1,2,32,128]{3,2,1,0:T(8,128)} copy(f32[1,2,32,128]{3,2,1,0:T(8,128)} %bitcast.3) | data formatting | bytes 65536
  26.9 1.3 %copy.14 = f32[32,128]{1,0:T(8,128)} copy(f32[32,128]{1,0:T(8,128)} %get-tuple-element.9) | data formatting | bytes 32768

commit v5 on v4

--- a/solution.py
+++ b/solution.py
@@ -99,7 +99,15 @@
     shift = BLK // LOOK_RG
     per_tile = BLK // shift
     per_part = per_tile // 2
-    part_steps = per_part // 4
+    part_steps = per_part // 2
+
+    barrier = pltpu.get_barrier_semaphore()
+
+    def greet(s, _):
+        pl.semaphore_signal(barrier, inc=1, device_id={"date": lax.rem(me + s, parties)}, device_id_type=MESH)
+        return 0
+
+    lax.fori_loop(1, parties, greet, 0)
 
     small = [
         pltpu.make_async_copy(source, target, small_sems.at[i])
@@ -125,14 +133,6 @@
         return 0
 
     lax.fori_loop(0, tiles_in, tile_start, 0)
-
-    barrier = pltpu.get_barrier_semaphore()
-
-    def greet(s, _):
-        pl.semaphore_signal(barrier, inc=1, device_id={"date": lax.rem(me + s, parties)}, device_id_type=MESH)
-        return 0
-
-    lax.fori_loop(1, parties, greet, 0)
 
     for copy in small[:3]:
         copy.wait()
@@ -268,12 +268,21 @@
             device_id={"date": twin}, device_id_type=MESH)
 
     def step(i, _):
-        for q in range(4):
-            resample(4 * i + q)
+        resample(2 * i)
+        resample(2 * i + 1)
 
         @pl.when(i == 1)
         def _():
-            lax.fori_loop(1, deep, z_pass, 0)
+            lax.fori_loop(0, 1, y_pass, 0)
+
+        @pl.when(i == 2)
+        def _():
+            lax.fori_loop(1, 2, z_pass, 0)
+
+        @pl.when(i == 3)
+        def _():
+            lax.fori_loop(2, deep, z_pass, 0)
+
 
         @pl.when(i % part_steps == part_steps - 1)
         def _():
@@ -293,7 +302,7 @@
 
         return 0
 
-    lax.fori_loop(0, blocks // 4, step, 0)
+    lax.fori_loop(0, blocks // 2, step, 0)
     def combine(b):
         m0, m1 = mg[b, 0].astype(jnp.float32), mg[b, 1].astype(jnp.float32)
         r0, r1 = res[b, 0].astype(jnp.float32), res[b, 1].astype(jnp.float32)
@@ -311,7 +320,7 @@
 
     combine_some(my_y, my_c)
     twin_wait(my_y)
-    lax.fori_loop(0, deep, y_pass, 0)
+    lax.fori_loop(1, deep, y_pass, 0)
     combine_some(my_y, 1 - my_c)
     combine_some(1 - my_y, my_c)
     twin_wait(1 - my_y)

time: 28.4 us -> 27.9 us (0.982)
  the two profiles are of different devices: /device:TPU:1 before, /device:TPU:0 now
where the time goes in v5:
time: 27.9 us; the launch traced here: 27.6 us
  Pallas kernels  24.3 us (87%)
  local copies, waits for them, and re-layouts  2.7 us (10%)
  between operations  0.64 us (2%)
    pallas_call x1, Pallas kernels, per_device(): pl.pallas_call(functools.partial(kernel, parties), out_shape=(jax.ShapeDt...  24.3 us
    unnamed x2, local copies, waits for them, and re-layouts  2.7 us

profile of v5, /device:TPU:0, one launch (start us, length us, event | category | flops | bytes accessed | tf_op | source)
XLA Modules:
  0.0 27.6 jit_solution(17635512705723899070)
XLA Ops:
  0.6 24.3 %coregister.1 = (f32[2,32,128]{2,1,0:T(8,128)}, f32[32,128]{1,0:T(8,128)}) custom-call(bf16[1,2,192,2112]{3,2,1,0:T(8,128)(2,1)} %x_hbm.1, bf16[2,128,128]{2,1,0:T(8,128)(2,1)} %master_hbm.1, f32[1,128]{1,0:T(1,128)} %bitcast.4, f32[1,128]{1,0:T(1,128)} %bitcast.5, s32[1,128]{1,0:T(1,128)} %row_pos_hbm.1, f32[1,128]{1,0:T(1,128)} %row_frac_hbm.1, ...), custom_call_target="tpu_custom_call" | custom-call | flops 600000000 | bytes 4000000 | tf_op jit(solution)/shard_map/coregister/pallas_call | solution.py:382
  24.9 1.4 %copy.13 = f32[1,2,32,128]{3,2,1,0:T(8,128)} copy(f32[1,2,32,128]{3,2,1,0:T(8,128)} %bitcast.3) | data formatting | bytes 65536
  26.3 1.3 %copy.14 = f32[32,128]{1,0:T(8,128)} copy(f32[32,128]{1,0:T(8,128)} %get-tuple-element.9) | data formatting | bytes 32768

commit v6 on v5

--- a/solution.py
+++ b/solution.py
@@ -169,7 +169,7 @@
 
     def m_copy(slot, peer, kind, tag):
         return pltpu.make_async_remote_copy(
-            src_ref=mg.at[slot], dst_ref=mg.at[slot], send_sem=m_s.at[kind, tag], recv_sem=m_r.at[slot],
+            src_ref=mg.at[slot], dst_ref=mg.at[slot], send_sem=m_s.at[kind], recv_sem=m_r.at[slot],
             device_id={"date": peer}, device_id_type=MESH)
 
     def z_index(s):
@@ -349,21 +349,11 @@
     for part in range(blocks // per_part):
         p_all(part).wait_send()
 
-    def z_sent(s, _):
-        peer = z_index(s) + my_y * 2 + my_c
-        m_copy(me, peer, 0, peer).wait_send()
-        return 0
-
-    def forward_sent(s, _):
-        near = z_index(s) + my_y * 2 + my_c
-        far = z_index(s) + (1 - my_y) * 2 + my_c
-        m_copy(near, across, 1, near).wait_send()
-        m_copy(near, twin, 2, near).wait_send()
-        m_copy(far, twin, 2, far).wait_send()
-        return 0
-
-    lax.fori_loop(1, deep, z_sent, 0)
-    lax.fori_loop(0, deep, forward_sent, 0)
+    for kind, count in enumerate((deep - 1, deep, 2 * deep)):
+        every = mg.at[pl.ds(0, count)]
+        pltpu.make_async_remote_copy(
+            src_ref=every, dst_ref=every, send_sem=m_s.at[kind], recv_sem=m_r.at[0],
+            device_id={"date": twin}, device_id_type=MESH).wait_send()
 
 
 def per_device(
@@ -413,7 +403,7 @@
             dma((8,)),
             dma((tiles_in + 1,)),
             dma, dma,
-            dma((3, parties)), dma((parties,)),
+            dma((3,)), dma((parties,)),
             dma((2 * tiles,)), dma((2 * tiles,)),
         ],
         compiler_params=pltpu.CompilerParams(

time: 27.9 us -> 27.4 us (0.982)
  Pallas kernels: 24.3 us -> 23.8 us
    pallas_call x1, Pallas kernels: 24.3 us -> 23.8 us  [per_device(): pl.pallas_call(functools.partial(kernel, parties), out_shape=(jax.ShapeDt...]
where the time goes in v6:
time: 27.4 us; the launch traced here: 27.1 us
  Pallas kernels  23.8 us (87%)
  local copies, waits for them, and re-layouts  2.7 us (10%)
  between operations  0.64 us (2%)
    pallas_call x1, Pallas kernels, per_device(): pl.pallas_call(functools.partial(kernel, parties), out_shape=(jax.ShapeDt...  23.8 us
    unnamed x2, local copies, waits for them, and re-layouts  2.7 us

profile of v6, /device:TPU:0, one launch (start us, length us, event | category | flops | bytes accessed | tf_op | source)
XLA Modules:
  0.0 27.1 jit_solution(369254937719973389)
XLA Ops:
  0.6 23.8 %coregister.1 = (f32[2,32,128]{2,1,0:T(8,128)}, f32[32,128]{1,0:T(8,128)}) custom-call(bf16[1,2,192,2112]{3,2,1,0:T(8,128)(2,1)} %x_hbm.1, bf16[2,128,128]{2,1,0:T(8,128)(2,1)} %master_hbm.1, f32[1,128]{1,0:T(1,128)} %bitcast.4, f32[1,128]{1,0:T(1,128)} %bitcast.5, s32[1,128]{1,0:T(1,128)} %row_pos_hbm.1, f32[1,128]{1,0:T(1,128)} %row_frac_hbm.1, ...), custom_call_target="tpu_custom_call" | custom-call | flops 600000000 | bytes 4000000 | tf_op jit(solution)/shard_map/coregister/pallas_call | solution.py:372
  24.4 1.4 %copy.13 = f32[1,2,32,128]{3,2,1,0:T(8,128)} copy(f32[1,2,32,128]{3,2,1,0:T(8,128)} %bitcast.3) | data formatting | bytes 65536
  25.8 1.3 %copy.14 = f32[32,128]{1,0:T(8,128)} copy(f32[32,128]{1,0:T(8,128)} %get-tuple-element.9) | data formatting | bytes 32768
